TPU v7x, 32 devices: a whole 2x2x4 slice. The times are simulated.
32 devices in a mesh: section: 2 (over y), batch: 16 (over z, x, core).
Axes of the slice: x: 2, y: 2, z: 4, core: 2. Of those that a mesh axis runs over, the one named last changes fastest.
Arguments:
- images: bfloat16 [32, 64, 3072], P('batch', None, 'section'), may hold values from -1 to 1
- noise_draw: bfloat16 [32, 64, 3072], P('batch', None, 'section'), may hold values from -6 to 6
- cotangent: bfloat16 [32, 64, 3072], P('batch', None, 'section'), may hold values from -6 to 6
- hue_angle: float32 [32], P('batch'), may hold values from -0.5 to 0.5
- saturation: float32 [32], P('batch'), may hold values from 0.5 to 1.5
- timestep: int32 [32], P('batch'), may hold values from 50 to 199
- stem_weight: bfloat16 [3072, 1024], P('section'), may hold values from -0.109375 to 0.109375
- conv_weight: bfloat16 [2, 9216, 1024], P('section', 'batch'), may hold values from -0.0625 to 0.0625
- emb_weight: bfloat16 [2, 1024, 2048], P('section'), may hold values from -0.1875 to 0.1875
- head_weight: bfloat16 [1024, 3072], P(None, 'section'), may hold values from -0.1875 to 0.1875
Outputs:
- purified: bfloat16 [32, 64, 3072], P('batch', None, 'section')
- colour_grad: float32 [32, 2], P('batch')
All inputs are finite; a program needn't handle non-finite values.
Results may differ from a plain program's by a relative error of at most 0.039.
Values may be sent and summed in bfloat16 or wider, within the bound.
A program may use at most 128 MiB of HBM per device.

v0:
```python
import math
import jax
import jax.numpy as jnp
from jax import lax
from jax.sharding import PartitionSpec as P

CH = 1024
GROUPS = 32
TEMB = 1024
GRID = 8
TSTEPS = 1000
PV = 3072


def shifted(value, axis, steps):
    count = lax.axis_size(axis)
    pairs = [(source, (source + steps) % count) for source in range(count)]
    return lax.ppermute(value, axis, pairs)


def from_root(block, axis, holder):
    block = jnp.where(lax.axis_index(axis) == holder, block, jnp.zeros_like(block))
    return lax.psum(block, axis)


def noise_levels(timestep):
    beta_rates = jnp.linspace(0.0001, 0.02, TSTEPS, dtype=jnp.float32)
    levels = jnp.cumprod(1.0 - beta_rates)
    chosen = jnp.arange(TSTEPS, dtype=jnp.int32)[None, :] == timestep[:, None]
    return jnp.sum(jnp.where(chosen, levels[None, :], jnp.float32(0.0)), axis=1)


def time_features(timestep):
    half_width = TEMB // 2
    frequency = jnp.exp(-math.log(10000.0) * jnp.arange(half_width, dtype=jnp.float32) / half_width)
    angles = timestep.astype(jnp.float32)[:, None] * frequency[None, :]
    return jax.nn.silu(jnp.concatenate([jnp.cos(angles), jnp.sin(angles)], axis=1)).astype(
        jnp.bfloat16
    )


def colour_maps(hue_angle, saturation):
    grey_map = jnp.full((3, 3), 1.0 / 3.0, dtype=jnp.float32)
    rotate_map = jnp.eye(3, dtype=jnp.float32) - grey_map
    cross_map = jnp.array(
        [[0.0, -1.0, 1.0], [1.0, 0.0, -1.0], [-1.0, 1.0, 0.0]], dtype=jnp.float32
    ) / math.sqrt(3.0)
    cosine = jnp.cos(hue_angle)[:, None, None]
    sine_of = jnp.sin(hue_angle)[:, None, None]
    turning = cosine * rotate_map + sine_of * cross_map
    sat_scale = saturation[:, None, None]
    matrix = grey_map + sat_scale * turning
    hue_slope = sat_scale * (cosine * cross_map - sine_of * rotate_map)
    return (matrix, hue_slope, turning)


def apply_map(matrix, pixels):
    return jnp.sum(matrix[:, None, None, :, :] * pixels[:, :, :, None, :], axis=-1)


def conv_branch(feature, weight, scaling):
    number = feature.shape[0]
    channels = feature.shape[2]
    grouped = feature.reshape(number, GRID * GRID, GROUPS, channels // GROUPS)
    centre = jnp.mean(grouped, axis=(1, 3), keepdims=True)
    spread_sq = jnp.mean(jnp.square(grouped - centre), axis=(1, 3), keepdims=True)
    normed = ((grouped - centre) * lax.rsqrt(spread_sq + 1e-05)).reshape(
        number, GRID * GRID, channels
    )
    factor = scaling[:, None, :channels]
    offset = scaling[:, None, channels:]
    active = jax.nn.silu(normed * (1.0 + factor) + offset).astype(jnp.bfloat16)
    padded = jnp.pad(active.reshape(number, GRID, GRID, channels), ((0, 0), (1, 1), (1, 1), (0, 0)))
    taps = [
        padded[:, row_tap : row_tap + GRID, col_tap : col_tap + GRID, :]
        for row_tap in range(3)
        for col_tap in range(3)
    ]
    columns = jnp.concatenate(taps, axis=-1).reshape(number * GRID * GRID, 9 * channels)
    product = jnp.dot(columns, weight, preferred_element_type=jnp.float32)
    return product.reshape(number, GRID * GRID, channels)


def residual_block(feature, weight, scaling):
    primal = feature.astype(jnp.float32)
    return (primal + conv_branch(primal, weight, scaling)).astype(jnp.bfloat16)


def block_adjoint(feature, weight, scaling, upstream):
    primal = feature.astype(jnp.float32)

    def branch_only(probe):
        return conv_branch(probe, weight, scaling)

    _, pullback = jax.vjp(branch_only, primal)
    upstream_f = upstream.astype(jnp.float32)
    return (upstream_f + pullback(upstream_f)[0]).astype(jnp.bfloat16)


def section_total(partial_sum):
    return lax.psum(partial_sum.astype(jnp.bfloat16), "section").astype(jnp.float32)


def send_forward(value):
    return shifted(value, "section", 1)


def send_backward(value):
    return shifted(value, "section", -1)


def spread(value, owner):
    return from_root(value, "section", owner)


def store_one(buffer, value, index_at, is_live):
    previous = lax.dynamic_index_in_dim(buffer, index_at, 0, keepdims=False)
    return lax.dynamic_update_index_in_dim(buffer, jnp.where(is_live, value, previous), index_at, 0)


def run_chain(position, entering, worker, sender):
    number = entering.shape[0]
    clocks = number + lax.axis_size("section") - 1

    def advance(clock, state_in):
        incoming, sources, results = state_in
        member = clock - position
        is_live = (member >= 0) & (member < number)
        index_at = jnp.clip(member, 0, number - 1)
        entry_row = lax.dynamic_index_in_dim(entering, index_at, 0, keepdims=False)
        source = jnp.where(position == 0, entry_row, incoming)

        def run_work():
            return worker(source, index_at)

        def pass_through():
            return source

        result = lax.cond(is_live, run_work, pass_through)
        sources = store_one(sources, source, index_at, is_live)
        results = store_one(results, result, index_at, is_live)
        return (sender(result), sources, results)

    start = (jnp.zeros_like(entering[0]), jnp.zeros_like(entering), jnp.zeros_like(entering))
    final_state = lax.fori_loop(0, clocks, advance, start)
    return (final_state[1], final_state[2])


def local(
    images,
    noise_draw,
    cotangent,
    hue_angle,
    saturation,
    timestep,
    stem_weight,
    conv_weight,
    emb_weight,
    head_weight,
):
    sections = lax.axis_size("section")
    place = lax.axis_index("section")
    number = images.shape[0]
    columns_here = images.shape[2]
    full_conv = lax.all_gather(conv_weight, "batch", axis=1, tiled=True)[0]
    level = noise_levels(timestep)
    root_level = jnp.sqrt(level)[:, None, None]
    root_noise = jnp.sqrt(1.0 - level)[:, None, None]
    matrix, hue_slope, sat_slope = colour_maps(hue_angle, saturation)
    pixels = images.astype(jnp.float32).reshape(number, GRID * GRID, columns_here // 3, 3)
    coloured = apply_map(matrix, pixels).reshape(number, GRID * GRID, columns_here)
    noised = root_level * coloured + root_noise * noise_draw.astype(jnp.float32)
    entry_part = jnp.dot(
        noised.astype(jnp.bfloat16).reshape(-1, columns_here),
        stem_weight,
        preferred_element_type=jnp.float32,
    )
    first = section_total(entry_part).astype(jnp.bfloat16).reshape(number, GRID * GRID, CH)
    offsets = jnp.dot(time_features(timestep), emb_weight[0], preferred_element_type=jnp.float32)

    def forward_work(source, index_at):
        scaling = lax.dynamic_slice_in_dim(offsets, index_at, 1, 0)
        return residual_block(source[None], full_conv, scaling)[0]

    fwd_inputs, fwd_outputs = run_chain(place, first, forward_work, send_forward)
    finals = spread(fwd_outputs, sections - 1)
    predicted = jnp.dot(finals.reshape(-1, CH), head_weight, preferred_element_type=jnp.float32)
    predicted = predicted.reshape(number, GRID * GRID, columns_here)
    purified = ((noised - root_noise * predicted) / root_level).astype(jnp.bfloat16)
    weighted = cotangent.astype(jnp.float32) * (1.0 / math.sqrt(GRID * GRID * PV))
    eps_grad = (-(root_noise / root_level) * weighted).astype(jnp.bfloat16)
    seed_part = lax.dot_general(
        eps_grad.reshape(-1, columns_here),
        head_weight,
        (((1,), (1,)), ((), ())),
        preferred_element_type=jnp.float32,
    )
    seed = section_total(seed_part).astype(jnp.bfloat16).reshape(number, GRID * GRID, CH)

    def adjoint_work(source, index_at):
        saved = lax.dynamic_index_in_dim(fwd_inputs, index_at, 0, keepdims=True)
        scaling = lax.dynamic_slice_in_dim(offsets, index_at, 1, 0)
        return block_adjoint(saved, full_conv, scaling, source[None])[0]

    back_inputs, back_outputs = run_chain(sections - 1 - place, seed, adjoint_work, send_backward)
    grads = spread(back_outputs, 0)
    stem_back = lax.dot_general(
        grads.reshape(-1, CH),
        stem_weight,
        (((1,), (1,)), ((), ())),
        preferred_element_type=jnp.float32,
    )
    stem_back = stem_back.reshape(number, GRID * GRID, columns_here)
    pixel_grad = (weighted + root_level * stem_back).reshape(
        number, GRID * GRID, columns_here // 3, 3
    )
    hue_part = jnp.sum(pixel_grad * apply_map(hue_slope, pixels), axis=(1, 2, 3))
    sat_part = jnp.sum(pixel_grad * apply_map(sat_slope, pixels), axis=(1, 2, 3))
    colour_grad = section_total(jnp.stack([hue_part, sat_part], axis=1))
    return (purified, colour_grad)


def solution(mesh):
    in_specs = (
        P("batch", None, "section"),
        P("batch", None, "section"),
        P("batch", None, "section"),
        P("batch"),
        P("batch"),
        P("batch"),
        P("section", None),
        P("section", "batch", None),
        P("section", None, None),
        P(None, "section"),
    )
    out_specs = (P("batch", None, "section"), P("batch", None))
    return jax.shard_map(local, mesh=mesh, in_specs=in_specs, out_specs=out_specs, check_vma=False)
```

profile of v0, /device:TPU:0, one launch (start us, length us, event | category | flops | bytes accessed | tf_op | source)
XLA Modules:
  0.0 400.9 jit_solution(12375936215744181771)
XLA Ops:
  8.9 3.1 copy.20
  12.0 3.4 copy.21
  15.4 3.4 multiply_reduce_fusion.2
  18.9 3.3 copy.22
  22.2 3.4 copy.23
  26.4 1.6 fusion.82
  28.1 3.2 convolution_convert_fusion.2
  31.3 1.9 convolution_convert_fusion.1
  34.0 3.4 fusion.58
  37.4 27.4 %all-reduce.18.cloned.1.call-done = (bf16[2,64,1024]{2,1,0:T(8,128)(2,1)}, bf16[2,64,1024]{2,1,0:T(8,128)(2,1)}) async-done(((bf16[2,64,1024]{2,1,0:T(8,128)(2,1)}, bf16[2,64,1024]{2,1,0:T(8,128)(2,1)}), (bf16[2,64,1024]{2,1,0:T(8,128)(2,1)}, bf16[2,64,1024]{2,1,0:T(8,128)(2,1)})) %all-reduce.18.cloned.1.call-update) | async-done | bytes 524304 | tf_op jit(solution)/shard_map/psum | solution.py:101
  64.8 72.1 %all-gather.2.cloned.1.call-done = bf16[1,9216,1024]{2,1,0:T(8,128)(2,1)} async-done(((bf16[1,576,1024]{2,1,0:T(8,128)(2,1)}), bf16[1,9216,1024]{2,1,0:T(8,128)(2,1)}) %all-gather.2.cloned.1.call-update) | async-done | bytes 18874384 | tf_op jit(solution)/shard_map/all_gather | solution.py:165
  138.3 72.6 %while.34 = (s32[]{:T(128)}, bf16[64,1024]{1,0:T(8,128)(2,1)}, bf16[2,64,1024]{2,1,0:T(8,128)(2,1)S(1)}, bf16[2,64,1024]{2,1,0:T(8,128)(2,1)}, s32[]{:T(128)}, /...) while((s32[]{:T(128)}, bf16[64,1024]{1,0:T(8,128)(2,1)}, ...), condition=%wide.region_12.13_spmd, body=%wide.region_5.12_spmd.sunk | while | flops 1210057728 | bytes 25409360 | solution.py:145
  138.3 1.0 bitcast_dynamic-update-slice_fusion.6
  139.3 18.3 %conditional.4 = (bf16[64,1024]{1,0:T(8,128)(2,1)S(1)}) conditional(s32[]{:T(128)} %convert_element_type.245, bf16[64,1024]{1,0:T(8,128)(2,1)S(1)} %get-tuple-element.587, (bf16[64,1024]{1,0:T(8,128)(2,1)S(1)}, s32[]{:T(128)}, f32[2,2048]{1,0:T(2,128)}, bf16[9216,1024]{1,0:T(8,128)(2,1)}) %tuple.116), branch_computations={%region_6.6_spmd, %region_7.11_spmd} | conditional | flops 1209861120 | bytes 23311430 | solution.py:139
  147.8 9.8 %fusion = bf16[64,1024]{1,0:T(8,128)(2,1)S(1)} fusion(bf16[64,9216]{1,0:T(8,128)(2,1)S(1)} %fusion.32, bf16[9216,1024]{1,0:T(8,128)(2,1)} %get-tuple-element.369, bf16[64,1024]{1,0:T(8,128)(2,1)S(1)} %get-tuple-element.366), kind=kOutput, calls=%fused_computation.1 | convolution fusion | flops 1208156160 | bytes 20316160 | tf_op jit(solution)/shard_map/while/body/eval_jaxpr/cond/branch_1_fun/dot_general | solution.py:80
  157.7 0.9 constant_dynamic-slice_fusion.7
  159.3 4.1 %collective-permute-done = bf16[64,1024]{1,0:T(8,128)(2,1)} collective-permute-done((bf16[64,1024]{1,0:T(8,128)(2,1)S(1)}, bf16[64,1024]{1,0:T(8,128)(2,1)}, u32[]{:S(2)}, u32[]{:S(2)}) %collective-permute-start) | collective-permute-done | bytes 131104 | tf_op jit(solution)/shard_map/while/body/eval_jaxpr/ppermute | solution.py:18
  163.5 1.0 bitcast_dynamic-update-slice_fusion.6
  164.5 18.3 %conditional.4 = (bf16[64,1024]{1,0:T(8,128)(2,1)S(1)}) conditional(s32[]{:T(128)} %convert_element_type.245, bf16[64,1024]{1,0:T(8,128)(2,1)S(1)} %get-tuple-element.587, (bf16[64,1024]{1,0:T(8,128)(2,1)S(1)}, s32[]{:T(128)}, f32[2,2048]{1,0:T(2,128)}, bf16[9216,1024]{1,0:T(8,128)(2,1)}) %tuple.116), branch_computations={%region_6.6_spmd, %region_7.11_spmd} | conditional | flops 1209861120 | bytes 23311430 | solution.py:139
  172.9 9.8 %fusion = bf16[64,1024]{1,0:T(8,128)(2,1)S(1)} fusion(bf16[64,9216]{1,0:T(8,128)(2,1)S(1)} %fusion.32, bf16[9216,1024]{1,0:T(8,128)(2,1)} %get-tuple-element.369, bf16[64,1024]{1,0:T(8,128)(2,1)S(1)} %get-tuple-element.366), kind=kOutput, calls=%fused_computation.1 | convolution fusion | flops 1208156160 | bytes 20316160 | tf_op jit(solution)/shard_map/while/body/eval_jaxpr/cond/branch_1_fun/dot_general | solution.py:80
  183.2 0.9 constant_dynamic-slice_fusion.7
  184.8 3.1 collective-permute-done
  187.9 1.0 bitcast_dynamic-update-slice_fusion.6
  188.9 19.0 %collective-permute-start = (bf16[64,1024]{1,0:T(8,128)(2,1)S(1)}, bf16[64,1024]{1,0:T(8,128)(2,1)}, u32[]{:S(2)}, u32[]{:S(2)}) collective-permute-start(bf16[64,1024]{1,0:T(8,128)(2,1)S(1)} %get-tuple-element.674), channel_id=1, source_target_pairs={{0,16},{16,0},{1,17},{17,1},{2,18},{18,2},{3,19},{19,3},{4,20},{20... | collective-permute-start | bytes 393224 | tf_op jit(solution)/shard_map/while/body/eval_jaxpr/ppermute | solution.py:18
  207.9 0.9 constant_dynamic-slice_fusion.7
  209.5 1.5 collective-permute-done
  212.3 138.6 %while.35 = (s32[]{:T(128)}, bf16[64,1024]{1,0:T(8,128)(2,1)}, bf16[2,64,1024]{2,1,0:T(8,128)(2,1)}, s32[]{:T(128)}, pred[]{:T(512)}, /*index=5*/bf16[2,64,1024]...) while((s32[]{:T(128)}, bf16[64,1024]{1,0:T(8,128)(2,1)}, ...), condition=%wide.region_28.29_spmd, body=%wide.region_15.28_spmd.sunk | while | flops 1212769664 | bytes 27270924 | solution.py:145
  212.3 1.0 bitcast_select_fusion.7
  213.3 42.1 %collective-permute-start.1 = (bf16[64,1024]{1,0:T(8,128)(2,1)S(1)}, bf16[64,1024]{1,0:T(8,128)(2,1)}, u32[]{:S(2)}, u32[]{:S(2)}) collective-permute-start(bf16[64,1024]{1,0:T(8,128)(2,1)S(1)} %get-tuple-element.675), channel_id=1, source_target_pairs={{0,16},{16,0},{1,17},{17,1},{2,18},{18,2},{3,19},{19,3},{4,20},{20... | collective-permute-start | bytes 393224 | tf_op jit(solution)/shard_map/while/body/eval_jaxpr/ppermute | solution.py:18
  255.4 0.9 constant_dynamic-slice_fusion.8
  257.0 1.4 collective-permute-done.1
  258.5 1.0 bitcast_select_fusion.7
  259.5 40.1 %conditional.5 = (bf16[64,1024]{1,0:T(8,128)(2,1)S(1)}) conditional(s32[]{:T(128)} %convert_element_type.246, bf16[64,1024]{1,0:T(8,128)(2,1)S(1)} %bitcast_select_fusion.7, (bf16[64,1024]{1,0:T(8,128)(2,1)S(1)}, bf16[9216,1024]{1,0:T(8,128)(2,1)}, s32[]{:T(128)}, bf16[2,64,1024]{2,1,0:T(8,128)(2,1)S(1)}, f32[2,2048]{1,0:T(2,128)}) %tuple.118), branch_computations={%region_16.16_spmd, %region_17.27_spmd} | conditional | flops 1212638592 | bytes 25697282 | solution.py:139
  267.2 13.2 %fusion.33 = bf16[1,8,8,9216]{3,2,1,0:T(8,128)(2,1)} fusion(bf16[64,1024]{1,0:T(8,128)(2,1)S(1)} %get-tuple-element.380, bf16[9216,1024]{1,0:T(8,128)(2,1)} %get-tuple-element.381), kind=kOutput, calls=%fused_computation.57 | convolution fusion | flops 1208549376 | bytes 20185088 | tf_op jit(solution)/shard_map/while/body/eval_jaxpr/cond/branch_1_fun/transpose(jvp())/dot_general | solution.py:80
  280.4 2.2 fusion.94
  282.6 0.9 pad_add_fusion
  284.3 3.0 multiply_reduce_fusion
  287.2 1.3 reduce_sum.142
  292.2 1.4 reduce_sum.154
  293.5 1.4 reduce_sum.155
  298.5 1.1 fusion.55
  299.6 2.0 collective-permute-start.1
  301.6 0.9 constant_dynamic-slice_fusion.8
  303.2 1.5 collective-permute-done.1
  304.7 1.0 bitcast_select_fusion.7
  305.7 40.1 %conditional.5 = (bf16[64,1024]{1,0:T(8,128)(2,1)S(1)}) conditional(s32[]{:T(128)} %convert_element_type.246, bf16[64,1024]{1,0:T(8,128)(2,1)S(1)} %bitcast_select_fusion.7, (bf16[64,1024]{1,0:T(8,128)(2,1)S(1)}, bf16[9216,1024]{1,0:T(8,128)(2,1)}, s32[]{:T(128)}, bf16[2,64,1024]{2,1,0:T(8,128)(2,1)S(1)}, f32[2,2048]{1,0:T(2,128)}) %tuple.118), branch_computations={%region_16.16_spmd, %region_17.27_spmd} | conditional | flops 1212638592 | bytes 25697282 | solution.py:139
  313.4 13.2 %fusion.33 = bf16[1,8,8,9216]{3,2,1,0:T(8,128)(2,1)} fusion(bf16[64,1024]{1,0:T(8,128)(2,1)S(1)} %get-tuple-element.380, bf16[9216,1024]{1,0:T(8,128)(2,1)} %get-tuple-element.381), kind=kOutput, calls=%fused_computation.57 | convolution fusion | flops 1208549376 | bytes 20185088 | tf_op jit(solution)/shard_map/while/body/eval_jaxpr/cond/branch_1_fun/transpose(jvp())/dot_general | solution.py:80
  326.6 2.2 fusion.94
  330.5 3.0 multiply_reduce_fusion
  333.5 1.3 reduce_sum.142
  338.4 1.4 reduce_sum.154
  339.7 1.4 reduce_sum.155
  344.7 1.1 fusion.55
  345.9 0.9 constant_dynamic-slice_fusion.8
  347.5 3.4 collective-permute-done.1
  350.9 1.7 broadcast_select_fusion
  353.3 3.3 copy.24
  356.6 3.4 copy.25
  360.0 3.3 copy.26
  363.3 3.4 copy.27
  366.7 14.6 %all-reduce.16.cloned.1.call-done = (bf16[2,64,1024]{2,1,0:T(8,128)(2,1)}, bf16[2,64,1024]{2,1,0:T(8,128)(2,1)}) async-done(((bf16[2,64,1024]{2,1,0:T(8,128)(2,1)}, bf16[2,64,1024]{2,1,0:T(8,128)(2,1)}), (bf16[2,64,1024]{2,1,0:T(8,128)(2,1)}, bf16[2,64,1024]{2,1,0:T(8,128)(2,1)})) %all-reduce.16.cloned.1.call-update) | async-done | bytes 524304 | tf_op jit(solution)/shard_map/psum | solution.py:23
  381.4 3.8 multiply_reduce_fusion.5
  385.2 4.9 %psum.39 = bf16[2,2]{0,1:T(2,128)(2,1)S(1)} all-reduce(bf16[2,2]{0,1:T(2,128)(2,1)S(1)} %pad_maximum_fusion.1), channel_id=1, replica_groups=mesh['section'=2,'batch'=16] {'section'}, use_global_device_ids=true, to_apply=%region_34.35 | all-reduce | flops 4 | bytes 16 | tf_op jit(solution)/shard_map/psum | solution.py:101
  390.8 2.7 fusion.79
  (157 shorter events, 60.5 us)
Async XLA Ops:
  8.0 23.3 %copy-start = (bf16[1024,1536]{1,0:T(8,128)(2,1)S(1)}, bf16[1024,1536]{1,0:T(8,128)(2,1)}, u32[]{:S(2)}) copy-start(bf16[1024,1536]{1,0:T(8,128)(2,1)} %param.28) | copy-start | bytes 9437188
  8.0 56.8 %all-reduce.18.cloned.1.call-start = ((), (), s32[]{:S(2)}) async-start(), calls=%async_computation.2 | async-start | bytes 1048576 | tf_op jit(solution)/shard_map/psum | solution.py:101
  12.0 3.4 copy-start.6
  12.0 3.4 copy-start.7
  22.2 4.0 %copy-start.8 = (s32[2]{0:T(128)S(1)}, s32[2]{0:T(128)}, u32[]{:S(2)}) copy-start(s32[2]{0:T(128)} %param.24) | copy-start | bytes 28
  26.4 4.8 %copy-start.2 = (f32[2]{0:T(128)}, f32[2]{0:T(128)S(1)}, u32[]{:S(2)}) copy-start(f32[2]{0:T(128)S(1)} %get-tuple-element.477) | copy-start | bytes 28
  26.4 4.8 %copy-start.4 = (f32[2]{0:T(128)}, f32[2]{0:T(128)S(1)}, u32[]{:S(2)}) copy-start(f32[2]{0:T(128)S(1)} %get-tuple-element.479) | copy-start | bytes 28
  33.1 103.8 %all-gather.2.cloned.1.call-start = ((), (), s32[]{:S(2)}) async-start(), calls=%async_computation | async-start | bytes 20054016 | tf_op jit(solution)/shard_map/all_gather | solution.py:165
  33.7 347.6 %all-reduce.16.cloned.1.call-start = ((), (), s32[]{:S(2)}) async-start(), calls=%async_computation.1 | async-start | bytes 1048576 | tf_op jit(solution)/shard_map/psum | solution.py:23
  157.6 5.8 %collective-permute-start = (bf16[64,1024]{1,0:T(8,128)(2,1)S(1)}, bf16[64,1024]{1,0:T(8,128)(2,1)}, u32[]{:S(2)}, u32[]{:S(2)}) collective-permute-start(bf16[64,1024]{1,0:T(8,128)(2,1)S(1)} %get-tuple-element.674), channel_id=1, source_target_pairs={{0,16},{16,0},{1,17},{17,1},{2,18},{18,2},{3,19},{19,3},{4,20},{20... | collective-permute-start | bytes 393224 | tf_op jit(solution)/shard_map/while/body/eval_jaxpr/ppermute | solution.py:18
  182.8 5.1 %collective-permute-start = (bf16[64,1024]{1,0:T(8,128)(2,1)S(1)}, bf16[64,1024]{1,0:T(8,128)(2,1)}, u32[]{:S(2)}, u32[]{:S(2)}) collective-permute-start(bf16[64,1024]{1,0:T(8,128)(2,1)S(1)} %get-tuple-element.674), channel_id=1, source_target_pairs={{0,16},{16,0},{1,17},{17,1},{2,18},{18,2},{3,19},{19,3},{4,20},{20... | collective-permute-start | bytes 393224 | tf_op jit(solution)/shard_map/while/body/eval_jaxpr/ppermute | solution.py:18
  188.9 22.0 %collective-permute-start = (bf16[64,1024]{1,0:T(8,128)(2,1)S(1)}, bf16[64,1024]{1,0:T(8,128)(2,1)}, u32[]{:S(2)}, u32[]{:S(2)}) collective-permute-start(bf16[64,1024]{1,0:T(8,128)(2,1)S(1)} %get-tuple-element.674), channel_id=1, source_target_pairs={{0,16},{16,0},{1,17},{17,1},{2,18},{18,2},{3,19},{19,3},{4,20},{20... | collective-permute-start | bytes 393224 | tf_op jit(solution)/shard_map/while/body/eval_jaxpr/ppermute | solution.py:18
  213.3 45.2 %collective-permute-start.1 = (bf16[64,1024]{1,0:T(8,128)(2,1)S(1)}, bf16[64,1024]{1,0:T(8,128)(2,1)}, u32[]{:S(2)}, u32[]{:S(2)}) collective-permute-start(bf16[64,1024]{1,0:T(8,128)(2,1)S(1)} %get-tuple-element.675), channel_id=1, source_target_pairs={{0,16},{16,0},{1,17},{17,1},{2,18},{18,2},{3,19},{19,3},{4,20},{20... | collective-permute-start | bytes 393224 | tf_op jit(solution)/shard_map/while/body/eval_jaxpr/ppermute | solution.py:18
  265.2 0.5 copy-start.1
  299.6 5.1 %collective-permute-start.1 = (bf16[64,1024]{1,0:T(8,128)(2,1)S(1)}, bf16[64,1024]{1,0:T(8,128)(2,1)}, u32[]{:S(2)}, u32[]{:S(2)}) collective-permute-start(bf16[64,1024]{1,0:T(8,128)(2,1)S(1)} %get-tuple-element.675), channel_id=1, source_target_pairs={{0,16},{16,0},{1,17},{17,1},{2,18},{18,2},{3,19},{19,3},{4,20},{20... | collective-permute-start | bytes 393224 | tf_op jit(solution)/shard_map/while/body/eval_jaxpr/ppermute | solution.py:18
  311.4 0.5 copy-start.1
  345.8 5.1 %collective-permute-start.1 = (bf16[64,1024]{1,0:T(8,128)(2,1)S(1)}, bf16[64,1024]{1,0:T(8,128)(2,1)}, u32[]{:S(2)}, u32[]{:S(2)}) collective-permute-start(bf16[64,1024]{1,0:T(8,128)(2,1)S(1)} %get-tuple-element.675), channel_id=1, source_target_pairs={{0,16},{16,0},{1,17},{17,1},{2,18},{18,2},{3,19},{19,3},{4,20},{20... | collective-permute-start | bytes 393224 | tf_op jit(solution)/shard_map/while/body/eval_jaxpr/ppermute | solution.py:18
  363.3 18.0 %copy-start.3 = (f32[2]{0:T(128)S(1)}, f32[2]{0:T(128)}, u32[]{:S(2)}) copy-start(f32[2]{0:T(128)} %copy-done.2) | copy-start | bytes 28
  381.4 9.4 %copy-start.5 = (f32[2]{0:T(128)S(1)}, f32[2]{0:T(128)}, u32[]{:S(2)}) copy-start(f32[2]{0:T(128)} %copy-done.4) | copy-start | bytes 28
Sparse Core Ops, SparseCore 0:
  33.3 31.5 all-reduce.17
  353.5 27.8 all-reduce.15
Sparse Core Ops, SparseCore 1:
  35.3 101.6 all-gather.1
where the time goes:
time: 404 us; the launch traced here: 401 us
  waiting for transfers between devices  130 us (32%)
  local copies, waits for them, and re-layouts  72.5 us (18%)
  starting transfers between devices  63.8 us (16%)
  matrix products  61.1 us (15%)
  other arithmetic  52.8 us (13%)
  between operations  15.6 us (4%)
  blocking collectives  4.94 us (1%)
    all_gather x1, waiting for transfers between devices, local(): full_conv = lax.all_gather(conv_weight, 'batch', axis=1, tiled=True)[0]  72.1 us
    ppermute x6, starting transfers between devices, shifted(): return lax.ppermute(value, axis, pairs)  63.6 us
    dot_general x4, matrix products, conv_branch(): product = jnp.dot(columns, weight, preferred_element_type=jnp.float32)  46.1 us
    psum x1, waiting for transfers between devices, section_total(): lax.psum(partial_sum.astype(jnp.bfloat16), 'section').astype(jnp.float32)  27.4 us
    reduce_sum x5, local copies, waits for them, and re-layouts, apply_map(): jnp.sum(matrix[:, None, None, :, :] * pixels[:, :, :, None, :], axis=-1)  16.7 us
    ppermute x6, waiting for transfers between devices, shifted(): return lax.ppermute(value, axis, pairs)  15.1 us
    psum x1, waiting for transfers between devices, from_root(): return lax.psum(block, axis)  14.6 us
    reduce_sum x8, other arithmetic, conv_branch(): grouped - centre  11.6 us
  transfers between devices with their start and end apart: 9, of which 9 were waited for; matrix products, arithmetic and copies ran while one was open for 7% of the time, Pallas kernels for 0%

commit v1 on v0

--- a/solution.py
+++ b/solution.py
@@ -20,7 +20,7 @@
 
 def from_root(block, axis, holder):
     block = jnp.where(lax.axis_index(axis) == holder, block, jnp.zeros_like(block))
-    return lax.psum(block, axis)
+    return jnp.sum(lax.all_gather(block, axis), axis=0)
 
 
 def noise_levels(timestep):

time: 404 us -> 393 us (0.973)
  waiting for transfers between devices: 130 us -> 103 us
  blocking collectives: 4.94 us -> 19.3 us
    psum x1 -> x0, waiting for transfers between devices: 14.6 us -> none  [from_root(): return lax.psum(block, axis)]
    all_gather x0 -> x2, blocking collectives: none -> 14.3 us  [from_root(): return jnp.sum(lax.all_gather(block, axis), axis=0)]
    psum x1, waiting for transfers between devices: 27.4 us -> 13.9 us  [section_total(): lax.psum(partial_sum.astype(jnp.bfloat16), 'section').astype(jnp.float32)]
  transfers between devices with their start and end apart: 9 -> 8, of which waited for: 9 -> 8; matrix products, arithmetic and copies ran while one was open for 7% -> 7% of each run, Pallas kernels for 0% -> 0%
where the time goes in v1:
time: 393 us; the launch traced here: 390 us
  waiting for transfers between devices  103 us (26%)
  local copies, waits for them, and re-layouts  72.7 us (18%)
  starting transfers between devices  64 us (16%)
  matrix products  61.1 us (16%)
  other arithmetic  54.7 us (14%)
  blocking collectives  19.3 us (5%)
  between operations  15.6 us (4%)
    all_gather x1, waiting for transfers between devices, local(): full_conv = lax.all_gather(conv_weight, 'batch', axis=1, tiled=True)[0]  72.1 us
    ppermute x6, starting transfers between devices, shifted(): return lax.ppermute(value, axis, pairs)  63.7 us
    dot_general x4, matrix products, conv_branch(): product = jnp.dot(columns, weight, preferred_element_type=jnp.float32)  46.1 us
    reduce_sum x5, local copies, waits for them, and re-layouts, apply_map(): jnp.sum(matrix[:, None, None, :, :] * pixels[:, :, :, None, :], axis=-1)  16.8 us
    ppermute x6, waiting for transfers between devices, shifted(): return lax.ppermute(value, axis, pairs)  16.2 us
    all_gather x2, blocking collectives, from_root(): return jnp.sum(lax.all_gather(block, axis), axis=0)  14.3 us
    psum x1, waiting for transfers between devices, section_total(): lax.psum(partial_sum.astype(jnp.bfloat16), 'section').astype(jnp.float32)  13.9 us
    reduce_sum x8, other arithmetic, conv_branch(): grouped - centre  11.7 us
  transfers between devices with their start and end apart: 8, of which 8 were waited for; matrix products, arithmetic and copies ran while one was open for 7% of the time, Pallas kernels for 0%

profile of v1, /device:TPU:0, one launch (start us, length us, event | category | flops | bytes accessed | tf_op | source)
XLA Modules:
  0.0 390.3 jit_solution(10560083627125310833)
XLA Ops:
  8.9 3.1 copy.26
  12.0 3.4 copy.27
  15.4 3.5 multiply_reduce_fusion.2
  18.9 3.3 copy.28
  22.2 3.4 copy.29
  26.5 1.6 fusion.82
  28.2 3.2 convolution_convert_fusion.2
  31.3 1.9 convolution_convert_fusion.1
  33.8 3.3 copy.30
  37.2 3.4 copy.31
  40.5 3.3 copy.32
  43.9 3.5 copy.33
  47.5 3.5 fusion.58
  51.0 13.9 %all-reduce.14.cloned.1.call-done = (bf16[2,64,1024]{2,1,0:T(8,128)(2,1)}, bf16[2,64,1024]{2,1,0:T(8,128)(2,1)}) async-done(((bf16[2,64,1024]{2,1,0:T(8,128)(2,1)}, bf16[2,64,1024]{2,1,0:T(8,128)(2,1)}), (bf16[2,64,1024]{2,1,0:T(8,128)(2,1)}, bf16[2,64,1024]{2,1,0:T(8,128)(2,1)})) %all-reduce.14.cloned.1.call-update) | async-done | bytes 524304 | tf_op jit(solution)/shard_map/psum | solution.py:101
  64.9 72.1 %all-gather.4.cloned.1.call-done = bf16[1,9216,1024]{2,1,0:T(8,128)(2,1)} async-done(((bf16[1,576,1024]{2,1,0:T(8,128)(2,1)}), bf16[1,9216,1024]{2,1,0:T(8,128)(2,1)}) %all-gather.4.cloned.1.call-update) | async-done | bytes 18874384 | tf_op jit(solution)/shard_map/all_gather | solution.py:165
  138.4 72.6 %while.34 = (s32[]{:T(128)}, bf16[64,1024]{1,0:T(8,128)(2,1)}, bf16[2,64,1024]{2,1,0:T(8,128)(2,1)S(1)}, bf16[2,64,1024]{2,1,0:T(8,128)(2,1)}, s32[]{:T(128)}, /...) while((s32[]{:T(128)}, bf16[64,1024]{1,0:T(8,128)(2,1)}, ...), condition=%wide.region_12.13_spmd, body=%wide.region_5.12_spmd.sunk | while | flops 1210057728 | bytes 25409360 | solution.py:145
  138.4 1.0 bitcast_dynamic-update-slice_fusion.6
  139.4 18.3 %conditional.4 = (bf16[64,1024]{1,0:T(8,128)(2,1)S(1)}) conditional(s32[]{:T(128)} %convert_element_type.249, bf16[64,1024]{1,0:T(8,128)(2,1)S(1)} %get-tuple-element.587, (bf16[64,1024]{1,0:T(8,128)(2,1)S(1)}, s32[]{:T(128)}, f32[2,2048]{1,0:T(2,128)}, bf16[9216,1024]{1,0:T(8,128)(2,1)}) %tuple.117), branch_computations={%region_6.6_spmd, %region_7.11_spmd} | conditional | flops 1209861120 | bytes 23311430 | solution.py:139
  147.9 9.8 %fusion = bf16[64,1024]{1,0:T(8,128)(2,1)S(1)} fusion(bf16[64,9216]{1,0:T(8,128)(2,1)S(1)} %fusion.32, bf16[9216,1024]{1,0:T(8,128)(2,1)} %get-tuple-element.369, bf16[64,1024]{1,0:T(8,128)(2,1)S(1)} %get-tuple-element.366), kind=kOutput, calls=%fused_computation.1 | convolution fusion | flops 1208156160 | bytes 20316160 | tf_op jit(solution)/shard_map/while/body/eval_jaxpr/cond/branch_1_fun/dot_general | solution.py:80
  157.8 0.9 constant_dynamic-slice_fusion.7
  159.4 4.1 %collective-permute-done = bf16[64,1024]{1,0:T(8,128)(2,1)} collective-permute-done((bf16[64,1024]{1,0:T(8,128)(2,1)S(1)}, bf16[64,1024]{1,0:T(8,128)(2,1)}, u32[]{:S(2)}, u32[]{:S(2)}) %collective-permute-start) | collective-permute-done | bytes 131104 | tf_op jit(solution)/shard_map/while/body/eval_jaxpr/ppermute | solution.py:18
  163.6 1.0 bitcast_dynamic-update-slice_fusion.6
  164.6 18.3 %conditional.4 = (bf16[64,1024]{1,0:T(8,128)(2,1)S(1)}) conditional(s32[]{:T(128)} %convert_element_type.249, bf16[64,1024]{1,0:T(8,128)(2,1)S(1)} %get-tuple-element.587, (bf16[64,1024]{1,0:T(8,128)(2,1)S(1)}, s32[]{:T(128)}, f32[2,2048]{1,0:T(2,128)}, bf16[9216,1024]{1,0:T(8,128)(2,1)}) %tuple.117), branch_computations={%region_6.6_spmd, %region_7.11_spmd} | conditional | flops 1209861120 | bytes 23311430 | solution.py:139
  173.0 9.8 %fusion = bf16[64,1024]{1,0:T(8,128)(2,1)S(1)} fusion(bf16[64,9216]{1,0:T(8,128)(2,1)S(1)} %fusion.32, bf16[9216,1024]{1,0:T(8,128)(2,1)} %get-tuple-element.369, bf16[64,1024]{1,0:T(8,128)(2,1)S(1)} %get-tuple-element.366), kind=kOutput, calls=%fused_computation.1 | convolution fusion | flops 1208156160 | bytes 20316160 | tf_op jit(solution)/shard_map/while/body/eval_jaxpr/cond/branch_1_fun/dot_general | solution.py:80
  184.9 3.1 collective-permute-done
  188.0 1.0 bitcast_dynamic-update-slice_fusion.6
  189.0 19.0 %collective-permute-start = (bf16[64,1024]{1,0:T(8,128)(2,1)S(1)}, bf16[64,1024]{1,0:T(8,128)(2,1)}, u32[]{:S(2)}, u32[]{:S(2)}) collective-permute-start(bf16[64,1024]{1,0:T(8,128)(2,1)S(1)} %get-tuple-element.672), channel_id=1, source_target_pairs={{0,16},{16,0},{1,17},{17,1},{2,18},{18,2},{3,19},{19,3},{4,20},{20... | collective-permute-start | bytes 393224 | tf_op jit(solution)/shard_map/while/body/eval_jaxpr/ppermute | solution.py:18
  208.0 0.9 constant_dynamic-slice_fusion.7
  209.6 1.4 collective-permute-done
  212.4 140.0 %while.35 = (s32[]{:T(128)}, bf16[64,1024]{1,0:T(8,128)(2,1)}, bf16[2,64,1024]{2,1,0:T(8,128)(2,1)}, s32[]{:T(128)}, pred[]{:T(512)}, /*index=5*/bf16[2,64,1024]...) while((s32[]{:T(128)}, bf16[64,1024]{1,0:T(8,128)(2,1)}, ...), condition=%wide.region_28.29_spmd, body=%wide.region_15.28_spmd.sunk | while | flops 1212769664 | bytes 27270924 | solution.py:145
  212.4 1.0 bitcast_select_fusion.7
  213.4 42.2 %collective-permute-start.1 = (bf16[64,1024]{1,0:T(8,128)(2,1)S(1)}, bf16[64,1024]{1,0:T(8,128)(2,1)}, u32[]{:S(2)}, u32[]{:S(2)}) collective-permute-start(bf16[64,1024]{1,0:T(8,128)(2,1)S(1)} %get-tuple-element.673), channel_id=1, source_target_pairs={{0,16},{16,0},{1,17},{17,1},{2,18},{18,2},{3,19},{19,3},{4,20},{20... | collective-permute-start | bytes 393224 | tf_op jit(solution)/shard_map/while/body/eval_jaxpr/ppermute | solution.py:18
  255.6 0.9 constant_dynamic-slice_fusion.8
  257.2 1.5 collective-permute-done.1
  258.7 1.0 bitcast_select_fusion.7
  259.7 40.2 %conditional.5 = (bf16[64,1024]{1,0:T(8,128)(2,1)S(1)}) conditional(s32[]{:T(128)} %convert_element_type.250, bf16[64,1024]{1,0:T(8,128)(2,1)S(1)} %bitcast_select_fusion.7, (bf16[64,1024]{1,0:T(8,128)(2,1)S(1)}, bf16[9216,1024]{1,0:T(8,128)(2,1)}, s32[]{:T(128)}, bf16[2,64,1024]{2,1,0:T(8,128)(2,1)S(1)}, f32[2,2048]{1,0:T(2,128)}) %tuple.119), branch_computations={%region_16.16_spmd, %region_17.27_spmd} | conditional | flops 1212638592 | bytes 25697282 | solution.py:139
  267.4 13.2 %fusion.33 = bf16[1,8,8,9216]{3,2,1,0:T(8,128)(2,1)} fusion(bf16[64,1024]{1,0:T(8,128)(2,1)S(1)} %get-tuple-element.380, bf16[9216,1024]{1,0:T(8,128)(2,1)} %get-tuple-element.381), kind=kOutput, calls=%fused_computation.57 | convolution fusion | flops 1208549376 | bytes 20185088 | tf_op jit(solution)/shard_map/while/body/eval_jaxpr/cond/branch_1_fun/transpose(jvp())/dot_general | solution.py:80
  280.6 2.3 fusion.94
  284.5 3.0 multiply_reduce_fusion
  287.5 1.3 reduce_sum.168
  292.4 1.3 reduce_sum.177
  293.7 1.4 reduce_sum.178
  298.8 1.1 fusion.55
  299.9 2.0 collective-permute-start.1
  303.5 1.5 collective-permute-done.1
  305.0 1.0 bitcast_select_fusion.7
  306.0 40.2 %conditional.5 = (bf16[64,1024]{1,0:T(8,128)(2,1)S(1)}) conditional(s32[]{:T(128)} %convert_element_type.250, bf16[64,1024]{1,0:T(8,128)(2,1)S(1)} %bitcast_select_fusion.7, (bf16[64,1024]{1,0:T(8,128)(2,1)S(1)}, bf16[9216,1024]{1,0:T(8,128)(2,1)}, s32[]{:T(128)}, bf16[2,64,1024]{2,1,0:T(8,128)(2,1)S(1)}, f32[2,2048]{1,0:T(2,128)}) %tuple.119), branch_computations={%region_16.16_spmd, %region_17.27_spmd} | conditional | flops 1212638592 | bytes 25697282 | solution.py:139
  313.7 13.2 %fusion.33 = bf16[1,8,8,9216]{3,2,1,0:T(8,128)(2,1)} fusion(bf16[64,1024]{1,0:T(8,128)(2,1)S(1)} %get-tuple-element.380, bf16[9216,1024]{1,0:T(8,128)(2,1)} %get-tuple-element.381), kind=kOutput, calls=%fused_computation.57 | convolution fusion | flops 1208549376 | bytes 20185088 | tf_op jit(solution)/shard_map/while/body/eval_jaxpr/cond/branch_1_fun/transpose(jvp())/dot_general | solution.py:80
  326.9 2.3 fusion.94
  330.8 3.0 multiply_reduce_fusion
  333.8 1.3 reduce_sum.168
  338.7 1.3 reduce_sum.177
  340.1 1.4 reduce_sum.178
  345.1 1.1 fusion.55
  346.3 0.9 constant_dynamic-slice_fusion.8
  347.9 4.5 %collective-permute-done.1 = bf16[64,1024]{1,0:T(8,128)(2,1)} collective-permute-done((bf16[64,1024]{1,0:T(8,128)(2,1)S(1)}, bf16[64,1024]{1,0:T(8,128)(2,1)}, u32[]{:S(2)}, u32[]{:S(2)}) %collective-permute-start.1) | collective-permute-done | bytes 131104 | tf_op jit(solution)/shard_map/while/body/eval_jaxpr/ppermute | solution.py:18
  352.4 1.0 broadcast_select_fusion
  353.4 7.2 %all-gather.1 = bf16[4,64,1024]{2,1,0:T(8,128)(2,1)} all-gather(bf16[2,64,1024]{2,1,0:T(8,128)(2,1)S(1)} %broadcast_select_fusion), channel_id=3, replica_groups=mesh['section'=2,'batch'=16] {'section'}, dimensions={0}, use_global_device_ids=true | all-gather | bytes 786432 | tf_op jit(solution)/shard_map/all_gather | solution.py:23
  360.5 1.9 reduce_sum.205
  362.4 3.8 multiply_reduce_fusion.5
  366.3 4.9 %psum.23 = bf16[2,2]{0,1:T(2,128)(2,1)S(1)} all-reduce(bf16[2,2]{0,1:T(2,128)(2,1)S(1)} %pad_maximum_fusion.1), channel_id=1, replica_groups=mesh['section'=2,'batch'=16] {'section'}, use_global_device_ids=true, to_apply=%region_34.35 | all-reduce | flops 4 | bytes 16 | tf_op jit(solution)/shard_map/psum | solution.py:101
  372.0 7.2 %all-gather = bf16[4,64,1024]{2,1,0:T(8,128)(2,1)} all-gather(bf16[2,64,1024]{2,1,0:T(8,128)(2,1)S(1)} %broadcast_select_fusion.1), channel_id=2, replica_groups=mesh['section'=2,'batch'=16] {'section'}, dimensions={0}, use_global_device_ids=true | all-gather | bytes 786432 | tf_op jit(solution)/shard_map/all_gather | solution.py:23
  379.1 1.1 reduce_sum.204
  380.3 2.6 fusion.79
  (160 shorter events, 62.5 us)
Async XLA Ops:
  8.0 23.3 %copy-start = (bf16[1024,1536]{1,0:T(8,128)(2,1)S(1)}, bf16[1024,1536]{1,0:T(8,128)(2,1)}, u32[]{:S(2)}) copy-start(bf16[1024,1536]{1,0:T(8,128)(2,1)} %param.28) | copy-start | bytes 9437188
  8.0 56.9 %all-reduce.14.cloned.1.call-start = ((), (), s32[]{:S(2)}) async-start(), calls=%async_computation.1 | async-start | bytes 1048576 | tf_op jit(solution)/shard_map/psum | solution.py:101
  12.0 3.4 copy-start.7
  12.0 3.4 copy-start.8
  22.2 4.1 %copy-start.9 = (s32[2]{0:T(128)S(1)}, s32[2]{0:T(128)}, u32[]{:S(2)}) copy-start(s32[2]{0:T(128)} %param.24) | copy-start | bytes 28
  26.5 4.8 %copy-start.3 = (f32[2]{0:T(128)}, f32[2]{0:T(128)S(1)}, u32[]{:S(2)}) copy-start(f32[2]{0:T(128)S(1)} %get-tuple-element.477) | copy-start | bytes 28
  26.5 4.8 %copy-start.5 = (f32[2]{0:T(128)}, f32[2]{0:T(128)S(1)}, u32[]{:S(2)}) copy-start(f32[2]{0:T(128)S(1)} %get-tuple-element.479) | copy-start | bytes 28
  33.2 103.8 %all-gather.4.cloned.1.call-start = ((), (), s32[]{:S(2)}) async-start(), calls=%async_computation | async-start | bytes 20054016 | tf_op jit(solution)/shard_map/all_gather | solution.py:165
  157.7 5.8 %collective-permute-start = (bf16[64,1024]{1,0:T(8,128)(2,1)S(1)}, bf16[64,1024]{1,0:T(8,128)(2,1)}, u32[]{:S(2)}, u32[]{:S(2)}) collective-permute-start(bf16[64,1024]{1,0:T(8,128)(2,1)S(1)} %get-tuple-element.672), channel_id=1, source_target_pairs={{0,16},{16,0},{1,17},{17,1},{2,18},{18,2},{3,19},{19,3},{4,20},{20... | collective-permute-start | bytes 393224 | tf_op jit(solution)/shard_map/while/body/eval_jaxpr/ppermute | solution.py:18
  182.9 5.1 %collective-permute-start = (bf16[64,1024]{1,0:T(8,128)(2,1)S(1)}, bf16[64,1024]{1,0:T(8,128)(2,1)}, u32[]{:S(2)}, u32[]{:S(2)}) collective-permute-start(bf16[64,1024]{1,0:T(8,128)(2,1)S(1)} %get-tuple-element.672), channel_id=1, source_target_pairs={{0,16},{16,0},{1,17},{17,1},{2,18},{18,2},{3,19},{19,3},{4,20},{20... | collective-permute-start | bytes 393224 | tf_op jit(solution)/shard_map/while/body/eval_jaxpr/ppermute | solution.py:18
  189.0 22.0 %collective-permute-start = (bf16[64,1024]{1,0:T(8,128)(2,1)S(1)}, bf16[64,1024]{1,0:T(8,128)(2,1)}, u32[]{:S(2)}, u32[]{:S(2)}) collective-permute-start(bf16[64,1024]{1,0:T(8,128)(2,1)S(1)} %get-tuple-element.672), channel_id=1, source_target_pairs={{0,16},{16,0},{1,17},{17,1},{2,18},{18,2},{3,19},{19,3},{4,20},{20... | collective-permute-start | bytes 393224 | tf_op jit(solution)/shard_map/while/body/eval_jaxpr/ppermute | solution.py:18
  213.4 45.3 %collective-permute-start.1 = (bf16[64,1024]{1,0:T(8,128)(2,1)S(1)}, bf16[64,1024]{1,0:T(8,128)(2,1)}, u32[]{:S(2)}, u32[]{:S(2)}) collective-permute-start(bf16[64,1024]{1,0:T(8,128)(2,1)S(1)} %get-tuple-element.673), channel_id=1, source_target_pairs={{0,16},{16,0},{1,17},{17,1},{2,18},{18,2},{3,19},{19,3},{4,20},{20... | collective-permute-start | bytes 393224 | tf_op jit(solution)/shard_map/while/body/eval_jaxpr/ppermute | solution.py:18
  265.4 0.5 copy-start.2
  299.9 5.1 %collective-permute-start.1 = (bf16[64,1024]{1,0:T(8,128)(2,1)S(1)}, bf16[64,1024]{1,0:T(8,128)(2,1)}, u32[]{:S(2)}, u32[]{:S(2)}) collective-permute-start(bf16[64,1024]{1,0:T(8,128)(2,1)S(1)} %get-tuple-element.673), channel_id=1, source_target_pairs={{0,16},{16,0},{1,17},{17,1},{2,18},{18,2},{3,19},{19,3},{4,20},{20... | collective-permute-start | bytes 393224 | tf_op jit(solution)/shard_map/while/body/eval_jaxpr/ppermute | solution.py:18
  311.7 0.5 copy-start.2
  346.2 6.2 %collective-permute-start.1 = (bf16[64,1024]{1,0:T(8,128)(2,1)S(1)}, bf16[64,1024]{1,0:T(8,128)(2,1)}, u32[]{:S(2)}, u32[]{:S(2)}) collective-permute-start(bf16[64,1024]{1,0:T(8,128)(2,1)S(1)} %get-tuple-element.673), channel_id=1, source_target_pairs={{0,16},{16,0},{1,17},{17,1},{2,18},{18,2},{3,19},{19,3},{4,20},{20... | collective-permute-start | bytes 393224 | tf_op jit(solution)/shard_map/while/body/eval_jaxpr/ppermute | solution.py:18
  352.4 10.0 %copy-start.4 = (f32[2]{0:T(128)S(1)}, f32[2]{0:T(128)}, u32[]{:S(2)}) copy-start(f32[2]{0:T(128)} %copy-done.3) | copy-start | bytes 28
  362.4 9.5 %copy-start.1 = (bf16[2,64,1024]{2,1,0:T(8,128)(2,1)S(1)}, bf16[2,64,1024]{2,1,0:T(8,128)(2,1)}, u32[]{:S(2)}) copy-start(bf16[2,64,1024]{2,1,0:T(8,128)(2,1)} %get-tuple-element.400) | copy-start | bytes 786436
  366.3 14.0 %copy-start.6 = (f32[2]{0:T(128)S(1)}, f32[2]{0:T(128)}, u32[]{:S(2)}) copy-start(f32[2]{0:T(128)} %copy-done.5) | copy-start | bytes 28
Sparse Core Ops, SparseCore 0:
  33.3 31.5 all-reduce.13
Sparse Core Ops, SparseCore 1:
  35.4 101.6 all-gather.3
